TPU v7x, 512 devices: a whole 4x4x16 slice. The times are simulated.
512 devices in a mesh: expert: 64 (over y, z), width: 8 (over x, core).
Axes of the slice: x: 4, y: 4, z: 16, core: 2. Of those that a mesh axis runs over, the one named last changes fastest.
Arguments:
- tokens: bfloat16 [4096, 6144], P('expert', 'width'), may hold values from -6 to 6
- expert_ids: int32 [4096, 8], P('expert'), may hold values from 0 to 383, all different within a row; in each aligned block of 64 rows (0 to 63, 64 to 127, ...) at most 2 rows name the same one
- route_weight: float32 [4096, 8], P('expert'), may hold values from 0.2 to 1.5
- gate_weight: bfloat16 [64, 6144, 1024], P('expert', None, 'width'), may hold values from -0.078125 to 0.078125
- up_weight: bfloat16 [64, 6144, 1024], P('expert', None, 'width'), may hold values from -0.078125 to 0.078125
- down_weight: bfloat16 [64, 6144, 1024], P('expert', None, 'width'), may hold values from -0.1875 to 0.1875
Outputs:
- mixed: bfloat16 [4096, 6144], P('expert', 'width')
Inputs may be any that keep to these rules, and one draw needn't show every extreme that they name: `expert_ids`: each row names 8 different experts. In each aligned block of 64 rows (the rows of one index of the expert axis) no expert is named by more than 2 rows.
All inputs are finite; a program needn't handle non-finite values.
Results may differ from a plain program's by a relative error of at most 0.014.
Values may be sent and summed in bfloat16 or wider, within the bound.
A program may use at most 64 MiB of HBM per device.

v0:
```python
import jax
import jax.numpy as jnp
from jax import lax
from jax.sharding import PartitionSpec as P

SEND = 2


def laid_out(parts, dim):
    parts = jnp.moveaxis(parts, 0, dim)
    dims = parts.shape
    return parts.reshape(*dims[:dim], dims[dim] * dims[dim + 1], *dims[dim + 2 :])


def copy_for_each(array, axis):
    copies = jnp.broadcast_to(array, (lax.axis_size(axis), *array.shape))
    return lax.all_to_all(copies, axis, split_axis=0, concat_axis=0, tiled=True)


def gather_directly(array, axis, dim):
    return laid_out(copy_for_each(array, axis), dim)


def cut_along(array, dim, size):
    dims = array.shape
    parts = array.reshape(*dims[:dim], size, dims[dim] // size, *dims[dim + 1 :])
    return jnp.moveaxis(parts, dim, 0)


def sum_at_owner(array, axis, dim):
    size = lax.axis_size(axis)
    parts = lax.all_to_all(cut_along(array, dim, size), axis, 0, 0, tiled=True)
    return jnp.sum(parts.astype(jnp.float32), axis=0)


def local_slots(route_ids, holders):
    experts_held = jnp.arange(holders, dtype=jnp.int32)
    route_hits = route_ids[:, :, None] == experts_held[None, None, :]
    matched = jnp.any(route_hits, axis=1).astype(jnp.int32)
    ranking = jnp.cumsum(matched, axis=0) - matched
    return (route_hits, matched, ranking)


def body(tokens, expert_ids, route_weight, gate_weight, up_weight, down_weight):
    holders = lax.axis_size("expert")
    tok_rows = tokens.shape[0]
    capacity = holders * SEND
    route_hits, matched, ranking = local_slots(expert_ids, holders)
    expert_base = jnp.arange(holders, dtype=jnp.int32)[None, :] * SEND
    slot_of = jnp.where(matched > 0, expert_base + ranking, capacity)
    row_number = jnp.broadcast_to(jnp.arange(tok_rows, dtype=jnp.int32)[:, None], slot_of.shape)
    slot_table = (
        jnp.full((capacity + 1,), tok_rows, jnp.int32)
        .at[slot_of.reshape(-1)]
        .set(row_number.reshape(-1))
    )
    outgoing = jnp.take(tokens, slot_table[:capacity], axis=0, mode="fill", fill_value=0)
    arrived = lax.all_to_all(
        outgoing.reshape(holders, SEND, outgoing.shape[1]),
        "expert",
        split_axis=0,
        concat_axis=0,
        tiled=True,
    )
    selected = arrived.reshape(capacity, arrived.shape[2])
    gate_mat = gate_weight[0]
    up_mat = up_weight[0]
    down_mat = down_weight[0]
    segment = gather_directly(selected, "width", 1)
    gate_val = jnp.dot(segment, gate_mat, preferred_element_type=jnp.float32)
    up_val = jnp.dot(segment, up_mat, preferred_element_type=jnp.float32)
    hidden = (jax.nn.silu(gate_val) * up_val).astype(jnp.bfloat16)
    weights_held = jnp.sum(jnp.where(route_hits, route_weight[:, :, None], 0.0), axis=1)
    slot_onehot = (ranking[:, :, None] == jnp.arange(SEND, dtype=jnp.int32)[None, None, :]) & (
        matched[:, :, None] > 0
    )
    coeff = (weights_held[:, :, None] * slot_onehot.astype(jnp.float32)).reshape(tok_rows, capacity)
    feature_rows = down_mat.shape[0] // lax.axis_size("width")
    summed = sum_at_owner(
        lax.dot_general(
            down_mat, hidden, (((1,), (1,)), ((), ())), preferred_element_type=jnp.float32
        ).astype(jnp.bfloat16),
        "width",
        0,
    )
    returned = lax.all_to_all(
        summed.reshape(feature_rows, holders, SEND).astype(jnp.bfloat16),
        "expert",
        split_axis=1,
        concat_axis=1,
        tiled=True,
    ).astype(jnp.float32)
    returned = returned.reshape(feature_rows, capacity)
    combined = lax.dot_general(
        coeff,
        returned,
        (((1,), (1,)), ((), ())),
        precision=lax.Precision.HIGHEST,
        preferred_element_type=jnp.float32,
    )
    return combined.astype(jnp.bfloat16)


def solution(mesh):
    in_specs = (
        P("expert", "width"),
        P("expert", None),
        P("expert", None),
        P("expert", None, "width"),
        P("expert", None, "width"),
        P("expert", None, "width"),
    )
    out_specs = P("expert", "width")
    return jax.shard_map(body, mesh=mesh, in_specs=in_specs, out_specs=out_specs, check_vma=False)
```

profile of v0, /device:TPU:8, one launch (start us, length us, event | category | flops | bytes accessed | tf_op | source)
XLA Modules:
  0.0 137.8 jit_solution(4852240698737620453)
XLA Ops:
  0.0 0.0 copy-start
  0.0 0.0 copy-start.1
  0.0 0.9 copy.18
  0.9 0.2 fusion.14
  1.1 0.1 reshape.119
  1.2 0.1 reduce_window_sum.11
  1.3 0.1 select_n.44
  1.4 15.5 %scatter_custom_fusion = s32[129]{0:T(256)S(1)} fusion(s32[4096]{0:T(1024)S(1)} %bitcast.37, s32[4096]{0:T(1024)S(1)} %reshape.119, s32[]{:T(128)} %constant.15.clone.1), kind=kCustom, calls=%fused_computation.40 | custom fusion | bytes 520 | tf_op jit(solution)/shard_map/scatter | solution.py:55
  17.0 0.1 slice.6
  17.1 0.0 copy-done.1
  17.1 0.9 gather_fusion
  18.0 0.1 gather.7
  18.1 0.3 broadcast_select_fusion
  18.3 36.6 %all_to_all.20 = bf16[64,2,768]{2,1,0:T(2,128)(2,1)S(1)} all-to-all(bf16[64,2,768]{2,1,0:T(2,128)(2,1)S(1)} %broadcast_select_fusion), channel_id=1, replica_groups=mesh['expert'=64,'width'=8] {'expert'}, dimensions={0} | all-to-all | bytes 393216 | tf_op jit(solution)/shard_map/all_to_all | solution.py:58
  55.0 0.1 reshape.104
  55.1 0.2 copy.20
  55.2 0.2 broadcast_in_dim.57
  55.4 0.0 copy-start.2
  55.5 26.0 %all_to_all.21 = bf16[8,128,768]{1,2,0:T(8,128)(2,1)S(1)} all-to-all(bf16[8,128,768]{1,2,0:T(8,128)(2,1)S(1)} %broadcast_in_dim.57), channel_id=1, replica_groups=mesh['expert'=64,'width'=8] {'width'}, dimensions={0} | all-to-all | bytes 3145728 | tf_op jit(solution)/shard_map/all_to_all | solution.py:17
  81.5 0.0 copy-done.2
  81.5 0.6 fusion.3
  82.1 0.0 copy-done
  82.1 3.7 %convolution_convert_fusion = bf16[128,6144]{1,0:T(8,128)(2,1)} fusion(bf16[1,6144,128]{2,1,0:T(8,128)(2,1)S(1)} %copy-done, bf16[128,6144]{0,1:T(8,128)(2,1)S(1)} %bitcast.34, bf16[1,6144,128]{2,1,0:T(8,128)(2,1)} %param.10, f32[128,128]{1,0:T(8,128)S(1)} %fusion.3), kind=kOutput, calls=%fused_computation.2 | convolution fusion | flops 403537920 | bytes 6356992 | tf_op jit(solution)/shard_map/dot_general | solution.py:80
  85.8 1.5 %copy.27 = bf16[16,8,8,768]{3,2,0,1:T(8,128)(2,1)S(1)} copy(bf16[16,8,8,768]{3,2,1,0:T(8,128)(2,1)} %bitcast.36) | data formatting | bytes 3145728 | tf_op jit(solution)/shard_map/reshape | solution.py:26
  87.3 24.2 %all_to_all.22 = bf16[8,768,128]{1,2,0:T(8,128)(2,1)S(1)} all-to-all(bf16[8,768,128]{1,2,0:T(8,128)(2,1)S(1)} %bitcast.35), channel_id=1, replica_groups=mesh['expert'=64,'width'=8] {'width'}, dimensions={0} | all-to-all | bytes 3145728 | tf_op jit(solution)/shard_map/all_to_all | solution.py:32
  111.6 0.0 copy-start.3
  111.6 0.2 reduce_sum.22
  111.8 0.7 convert_element_type.42
  112.6 6.6 %all-to-all-start.3 = ((bf16[768,64,2]{0,2,1:T(2,128)(2,1)}), bf16[768,64,2]{0,2,1:T(2,128)(2,1)S(1)}, u32[]{:S(2)}, u32[]{:S(2)}) async-start(bf16[768,64,2]{0,2,1:T(2,128)(2,1)} %convert_element_type.42), calls=%async_computation.3 | async-start | bytes 393216 | tf_op jit(solution)/shard_map/all_to_all | solution.py:86
  119.1 0.0 copy-done.3
  119.1 0.1 copy.19
  119.2 0.2 select_reduce_fusion
  119.4 17.4 %all-to-all-done.3 = bf16[768,64,2]{0,2,1:T(2,128)(2,1)S(1)} async-done(((bf16[768,64,2]{0,2,1:T(2,128)(2,1)}), bf16[768,64,2]{0,2,1:T(2,128)(2,1)S(1)}, u32[]{:S(2)}, u32[]{:S(2)}) %all-to-all-start.3) | async-done | bytes 196640 | tf_op jit(solution)/shard_map/all_to_all | solution.py:86
  136.8 0.9 fusion.5
  (8 shorter events, 0.1 us)
Async XLA Ops:
  0.0 82.1 %copy-start = (bf16[1,6144,128]{2,1,0:T(8,128)(2,1)S(1)}, bf16[1,6144,128]{2,1,0:T(8,128)(2,1)}, u32[]{:S(2)}) copy-start(bf16[1,6144,128]{2,1,0:T(8,128)(2,1)} %param.11) | copy-start | bytes 4718596
  0.0 17.1 %copy-start.1 = (bf16[64,768]{1,0:T(8,128)(2,1)S(1)}, bf16[64,768]{1,0:T(8,128)(2,1)}, u32[]{:S(2)}) copy-start(bf16[64,768]{1,0:T(8,128)(2,1)} %param.6) | copy-start | bytes 294916
  55.4 26.1 %copy-start.2 = (bf16[1,6144,128]{2,1,0:T(8,128)(2,1)S(1)}, bf16[1,6144,128]{2,1,0:T(8,128)(2,1)}, u32[]{:S(2)}) copy-start(bf16[1,6144,128]{2,1,0:T(8,128)(2,1)} %param.9) | copy-start | bytes 4718596
  111.6 7.6 %copy-start.3 = (f32[64,8]{0,1:T(8,128)S(1)}, f32[64,8]{0,1:T(8,128)}, u32[]{:S(2)}) copy-start(f32[64,8]{0,1:T(8,128)} %param.8) | copy-start | bytes 6148
  112.6 24.3 %all-to-all-start.3 = ((bf16[768,64,2]{0,2,1:T(2,128)(2,1)}), bf16[768,64,2]{0,2,1:T(2,128)(2,1)S(1)}, u32[]{:S(2)}, u32[]{:S(2)}) async-start(bf16[768,64,2]{0,2,1:T(2,128)(2,1)} %convert_element_type.42), calls=%async_computation.3 | async-start | bytes 393216 | tf_op jit(solution)/shard_map/all_to_all | solution.py:86
where the time goes:
time: 138 us
  blocking collectives  86.9 us (63%)
  local copies, waits for them, and re-layouts  20.5 us (15%)
  waiting for transfers between devices  17.4 us (13%)
  starting transfers between devices  6.57 us (5%)
  matrix products  5.24 us (4%)
    all_to_all x1, blocking collectives, body(): lax.all_to_all(outgoing.reshape(holders, SEND, outgoing.shape[1]), 'exper...  36.6 us
    all_to_all x1, blocking collectives, copy_for_each(): return lax.all_to_all(copies, axis, split_axis=0, concat_axis=0, tiled=True)  26 us
    all_to_all x1, blocking collectives, sum_at_owner(): parts = lax.all_to_all(cut_along(array, dim, size), axis, 0, 0, tiled=True)  24.2 us
    all_to_all x1, waiting for transfers between devices, body(): lax.all_to_all(summed.reshape(feature_rows, holders, SEND).astype(jnp.bfl...  17.4 us
    scatter x1, local copies, waits for them, and re-layouts, body(): slot_table = jnp.full((capacity + 1,), tok_rows, jnp.int32).at[slot_of.re...  15.5 us
    all_to_all x1, starting transfers between devices, body(): lax.all_to_all(summed.reshape(feature_rows, holders, SEND).astype(jnp.bfl...  6.57 us
    dot_general x1, matrix products, body(): lax.dot_general(down_mat, hidden, (((1,), (1,)), ((), ())), preferred_ele...  3.69 us
  transfers between devices with their start and end apart: 1, of which 1 were waited for; matrix products, arithmetic and copies ran while one was open for 0% of the time, Pallas kernels for 0%

commit v1 on v0

v1 whole, which is shorter than its diff:
```python
import jax
import jax.numpy as jnp
from jax import lax
from jax.experimental import pallas as pl
from jax.experimental.pallas import tpu as pltpu
from jax.sharding import PartitionSpec as P

MESH = pl.DeviceIdType.MESH
BF16 = jnp.bfloat16
F32 = jnp.float32
Y, Z, X = 4, 16, 4
SEND = 2
SLOTS = Y * Z * SEND
TOK, FEAT, FF = 64, 768, 128
D = FEAT * X * 2
NC = 3
F = FEAT // NC
HALF = Z // 2
ROWS = SLOTS // 2


def dot(a, b, dims=((1,), (0,))):
    return lax.dot_general(a, b, (dims, ((), ())), preferred_element_type=F32)


def iota(shape, dim):
    return lax.broadcasted_iota(jnp.int32, shape, dim)


def wait_bytes(ref, sem):
    pltpu.make_async_copy(ref, ref, sem).wait()


def kernel(
    tok, ids, rw, wg_hbm, wu_hbm, wd_hbm, out,
    wgu, wd, ysend, yrecv, zsend, xall, psend, precv, opp_out, opp_in,
    nbr_out, nbr_in, sums, zsend2, zrecv2, ysend2, yrecv2,
    w_sem, y_ssem, y_rsem, z_ssem, z_rsem, g_ssem, g_rsem, p_ssem, p_rsem,
    o_ssem, o_rsem, n_ssem, n_rsem, z2_ssem, z2_rsem, y2_ssem, y2_rsem,
):
    e, w = lax.axis_index("expert"), lax.axis_index("width")
    y, z = e // Z, e % Z
    x, core = w // 2, w % 2
    partner = x * 2 + (1 - core)
    xl, xr, xo = (x + X - 1) % X, (x + 1) % X, (x + 2) % X
    left, right, oppo = xl * 2 + core, xr * 2 + core, xo * 2 + core

    def ypeer(d):
        return (y + d) % Y

    def zpeer(d):
        return (z + d) % Z

    zorder = [8, 7, 9, 6, 10, 5, 11, 4, 12, 3, 13, 2, 14, 1, 15]

    weights = [
        pltpu.make_async_copy(wg_hbm.at[0], wgu.at[:, pl.ds(0, FF)], w_sem.at[0]),
        pltpu.make_async_copy(wu_hbm.at[0], wgu.at[:, pl.ds(FF, FF)], w_sem.at[1]),
        pltpu.make_async_copy(wd_hbm.at[0], wd, w_sem.at[2]),
    ]

    bar = pltpu.get_barrier_semaphore()

    def greet(ee, ww):
        pl.semaphore_signal(bar, inc=1, device_id=(ee, ww), device_id_type=MESH)

    for d in zorder:
        greet(y * Z + zpeer(d), w)
    for d in range(1, Y):
        greet(ypeer(d) * Z + z, w)
    for ww in (left, right, partner):
        greet(e, ww)
    for copy in weights:
        copy.start()

    def remote(src, dst, ssem, rsem, ee, ww):
        pltpu.make_async_remote_copy(
            src_ref=src, dst_ref=dst, send_sem=ssem, recv_sem=rsem,
            device_id=(ee, ww), device_id_type=MESH,
        ).start()

    column = iota((TOK, SLOTS), 1)
    expert = lax.shift_right_logical(column, 1)
    match = jnp.zeros((TOK, SLOTS), F32)
    weight = jnp.zeros((TOK, SLOTS), F32)
    for k in range(ids.shape[1]):
        hit = ids[:, k : k + 1] == expert
        match = jnp.where(hit, 1.0, match)
        weight = jnp.where(hit, rw[:, k : k + 1], weight)
    earlier = jnp.where(iota((TOK, TOK), 1) < iota((TOK, TOK), 0), 1.0, 0.0).astype(BF16)
    rank = dot(earlier, match.astype(BF16))
    chosen = jnp.where(rank == (column & 1).astype(F32), match, 0.0)
    coeff = weight * chosen
    coeff_hi = coeff.astype(BF16)
    coeff_lo = (coeff - coeff_hi.astype(F32)).astype(BF16)
    outgoing = dot(chosen.astype(BF16), tok[...], ((0,), (0,)))
    for c in range(NC):
        ysend[c] = outgoing[:, c * F : (c + 1) * F].astype(BF16).reshape(Y, Z * SEND, F)

    def order(a, b):
        return (
            lax.shift_left((lax.shift_right_logical(a, 1) & 3), 5)
            + lax.shift_left(lax.shift_right_logical(a, 3), 1)
            + (a & 1)
        ) == b

    i0, i1 = iota((SLOTS, SLOTS), 0), iota((SLOTS, SLOTS), 1)
    to_z = jnp.where(order(i0, i1), 1.0, 0.0).astype(BF16)
    to_y = jnp.where(order(i1, i0), 1.0, 0.0).astype(BF16)

    pl.semaphore_wait(bar, len(zorder) + (Y - 1) + 3)

    for c in range(NC):
        for d in (2, 1, 3):
            remote(ysend.at[c, ypeer(d)], yrecv.at[c, y], y_ssem, y_rsem.at[c], ypeer(d) * Z + z, w)
        pltpu.make_async_copy(ysend.at[c, y], yrecv.at[c, y], y_rsem.at[c]).start()

    for c in range(NC):
        wait_bytes(yrecv.at[c], y_rsem.at[c])
        zsend[c] = dot(to_z, yrecv[c].reshape(SLOTS, F)).astype(BF16).reshape(Z, Y * SEND, F)
        for d in zorder:
            remote(zsend.at[c, zpeer(d)], xall.at[c, w, z], z_ssem, z_rsem.at[c], y * Z + zpeer(d), w)
        pltpu.make_async_copy(zsend.at[c, z], xall.at[c, w, z], z_rsem.at[c]).start()

    lower, upper = pl.ds(0, HALF), pl.ds(HALF, HALF)

    def give(c, ref, k, ww):
        remote(ref, ref, g_ssem, g_rsem.at[c, k], e, ww)

    def own(c):
        wait_bytes(xall.at[c, w], z_rsem.at[c])
        give(c, xall.at[c, w], 0, right)
        give(c, xall.at[c, w], 1, left)
        give(c, xall.at[c, w], 4, partner)

    def forward(c):
        wait_bytes(xall.at[c, left], g_rsem.at[c, 0])
        give(c, xall.at[c, left, lower], 2, right)
        give(c, xall.at[c, left], 5, partner)
        wait_bytes(xall.at[c, right], g_rsem.at[c, 1])
        give(c, xall.at[c, right, upper], 3, left)
        give(c, xall.at[c, right], 6, partner)

    def opposite(c):
        wait_bytes(xall.at[c, oppo, lower], g_rsem.at[c, 2])
        wait_bytes(xall.at[c, oppo, upper], g_rsem.at[c, 3])
        give(c, xall.at[c, oppo], 7, partner)

    def gathered(c):
        wait_bytes(xall.at[c, partner], g_rsem.at[c, 4])
        wait_bytes(xall.at[c, xl * 2 + 1 - core], g_rsem.at[c, 5])
        wait_bytes(xall.at[c, xr * 2 + 1 - core], g_rsem.at[c, 6])
        wait_bytes(xall.at[c, xo * 2 + 1 - core], g_rsem.at[c, 7])

    def project(c, total):
        for ww in range(2 * X):
            rows = pl.ds(ww * FEAT + c * F, F)
            total = total + dot(xall[c, ww].reshape(SLOTS, F), wgu[rows, :])
        return total

    total = jnp.zeros((SLOTS, 2 * FF), F32)
    own(0)
    forward(0)
    for c in range(NC):
        if c + 1 < NC:
            own(c + 1)
        opposite(c)
        if c + 1 < NC:
            forward(c + 1)
        gathered(c)
        if c == 0:
            weights[0].wait()
            weights[1].wait()
        total = project(c, total)
    gate, up = total[:, :FF], total[:, FF:]
    hidden = (gate / (1.0 + jnp.exp(-gate)) * up).astype(BF16)
    weights[2].wait()

    def part(c, ww):
        rows = pl.ds(pl.multiple_of(ww * FEAT + c * F, F), F)
        return dot(hidden, wd[rows, :], ((1,), (1,)))

    def to_partner(c):
        for xx in range(X):
            psend[c, xx] = part(c, xx * 2 + 1 - core).astype(BF16)
        remote(psend.at[c], precv.at[c], p_ssem, p_rsem.at[c], e, partner)

    def add_cores(c):
        wait_bytes(precv.at[c], p_rsem.at[c])
        total = part(c, oppo) + precv[c, xo].astype(F32)
        opp_out[c] = total.astype(BF16).reshape(2, ROWS, F)
        remote(opp_out.at[c, 0], opp_in.at[c, 0], o_ssem, o_rsem.at[c, 0], e, right)
        remote(opp_out.at[c, 1], opp_in.at[c, 1], o_ssem, o_rsem.at[c, 1], e, left)
        sums[c, 0] = part(c, right) + precv[c, xr].astype(F32)
        sums[c, 1] = part(c, left) + precv[c, xl].astype(F32)
        sums[c, 2] = part(c, w) + precv[c, x].astype(F32)

    def to_neighbours(c):
        a, b = pl.ds(0, ROWS), pl.ds(ROWS, ROWS)
        wait_bytes(opp_in.at[c, 0], o_rsem.at[c, 0])
        nbr_out[c, 0, a] = (sums[c, 0, a] + opp_in[c, 0].astype(F32)).astype(BF16)
        nbr_out[c, 0, b] = sums[c, 0, b].astype(BF16)
        remote(nbr_out.at[c, 0], nbr_in.at[c, 0], n_ssem, n_rsem.at[c, 0], e, right)
        wait_bytes(opp_in.at[c, 1], o_rsem.at[c, 1])
        nbr_out[c, 1, a] = sums[c, 1, a].astype(BF16)
        nbr_out[c, 1, b] = (sums[c, 1, b] + opp_in[c, 1].astype(F32)).astype(BF16)
        remote(nbr_out.at[c, 1], nbr_in.at[c, 1], n_ssem, n_rsem.at[c, 1], e, left)

    def back_z(c):
        wait_bytes(nbr_in.at[c, 0], n_rsem.at[c, 0])
        wait_bytes(nbr_in.at[c, 1], n_rsem.at[c, 1])
        total = sums[c, 2] + nbr_in[c, 0].astype(F32) + nbr_in[c, 1].astype(F32)
        zsend2[c] = total.astype(BF16).reshape(Z, Y * SEND, F)
        for d in zorder:
            remote(zsend2.at[c, zpeer(d)], zrecv2.at[c, z], z2_ssem, z2_rsem.at[c], y * Z + zpeer(d), w)
        pltpu.make_async_copy(zsend2.at[c, z], zrecv2.at[c, z], z2_rsem.at[c]).start()

    def back_y(c):
        wait_bytes(zrecv2.at[c], z2_rsem.at[c])
        ysend2[c] = dot(to_y, zrecv2[c].reshape(SLOTS, F)).astype(BF16).reshape(Y, Z * SEND, F)
        for d in (2, 1, 3):
            remote(ysend2.at[c, ypeer(d)], yrecv2.at[c, y], y2_ssem, y2_rsem.at[c], ypeer(d) * Z + z, w)
        pltpu.make_async_copy(ysend2.at[c, y], yrecv2.at[c, y], y2_rsem.at[c]).start()

    def combine(c):
        wait_bytes(yrecv2.at[c], y2_rsem.at[c])
        returned = yrecv2[c].reshape(SLOTS, F)
        mixed = dot(coeff_hi, returned) + dot(coeff_lo, returned)
        out[:, c * F : (c + 1) * F] = mixed.astype(BF16)

    steps = [to_partner, add_cores, to_neighbours, back_z, back_y, combine]
    at = [0, 1, 2.5, 4, 7, 8.5]
    plan = sorted((at[s] + 1.5 * c, s, c) for s in range(len(steps)) for c in range(NC))
    for _, s, c in plan:
        steps[s](c)

    wait_bytes(ysend.at[:, pl.ds(0, Y - 1)], y_ssem)
    wait_bytes(zsend.at[:, pl.ds(0, Z - 1)], z_ssem)
    wait_bytes(xall.at[:, pl.ds(0, 7)], g_ssem)
    wait_bytes(psend, p_ssem)
    wait_bytes(opp_out, o_ssem)
    wait_bytes(nbr_out, n_ssem)
    wait_bytes(zsend2.at[:, pl.ds(0, Z - 1)], z2_ssem)
    wait_bytes(ysend2.at[:, pl.ds(0, Y - 1)], y2_ssem)


def body(tokens, expert_ids, route_weight, gate_weight, up_weight, down_weight):
    vmem = pl.BlockSpec(memory_space=pltpu.VMEM)
    hbm = pl.BlockSpec(memory_space=pl.ANY)
    dma = pltpu.SemaphoreType.DMA
    return pl.pallas_call(
        kernel,
        out_shape=jax.ShapeDtypeStruct((TOK, FEAT), BF16),
        in_specs=[vmem, vmem, vmem, hbm, hbm, hbm],
        out_specs=vmem,
        scratch_shapes=[
            pltpu.VMEM((D, 2 * FF), BF16),
            pltpu.VMEM((D, FF), BF16),
            pltpu.VMEM((NC, Y, Z * SEND, F), BF16),
            pltpu.VMEM((NC, Y, Z * SEND, F), BF16),
            pltpu.VMEM((NC, Z, Y * SEND, F), BF16),
            pltpu.VMEM((NC, 2 * X, Z, Y * SEND, F), BF16),
            pltpu.VMEM((NC, X, SLOTS, F), BF16),
            pltpu.VMEM((NC, X, SLOTS, F), BF16),
            pltpu.VMEM((NC, 2, ROWS, F), BF16),
            pltpu.VMEM((NC, 2, ROWS, F), BF16),
            pltpu.VMEM((NC, 2, SLOTS, F), BF16),
            pltpu.VMEM((NC, 2, SLOTS, F), BF16),
            pltpu.VMEM((NC, 3, SLOTS, F), F32),
            pltpu.VMEM((NC, Z, Y * SEND, F), BF16),
            pltpu.VMEM((NC, Z, Y * SEND, F), BF16),
            pltpu.VMEM((NC, Y, Z * SEND, F), BF16),
            pltpu.VMEM((NC, Y, Z * SEND, F), BF16),
            dma((3,)),
            dma, dma((NC,)), dma, dma((NC,)), dma, dma((NC, 8)), dma, dma((NC,)),
            dma, dma((NC, 2)), dma, dma((NC, 2)), dma, dma((NC,)), dma, dma((NC,)),
        ],
        compiler_params=pltpu.CompilerParams(
            collective_id=0, has_side_effects=True, vmem_limit_bytes=40 * 2**20
        ),
        cost_estimate=pl.CostEstimate(flops=6 * SLOTS * D * FF, bytes_accessed=6 * D * FF, transcendentals=SLOTS * FF),
        name="experts",
    )(tokens, expert_ids, route_weight, gate_weight, up_weight, down_weight)


def solution(mesh):
    in_specs = (
        P("expert", "width"),
        P("expert", None),
        P("expert", None),
        P("expert", None, "width"),
        P("expert", None, "width"),
        P("expert", None, "width"),
    )
    out_specs = P("expert", "width")
    return jax.shard_map(body, mesh=mesh, in_specs=in_specs, out_specs=out_specs, check_vma=False)
```

time: 138 us -> 78 us (0.57)
  the two profiles are of different devices: /device:TPU:8 before, /device:TPU:4 now
where the time goes in v1:
time: 78 us; the launch traced here: 77.7 us
  Pallas kernels  70.4 us (90%)
  local copies, waits for them, and re-layouts  7.3 us (9%)
    pallas_call x1, Pallas kernels, body(): pl.pallas_call(kernel, out_shape=jax.ShapeDtypeStruct((TOK, FEAT), BF16),...  70.4 us
    unnamed x11, local copies, waits for them, and re-layouts  7.3 us

profile of v1, /device:TPU:4, one launch (start us, length us, event | category | flops | bytes accessed | tf_op | source)
XLA Modules:
  0.0 77.7 jit_solution(10006614237743525443)
XLA Ops:
  0.0 0.8 copy.7.ids
  0.8 0.8 copy.8.rw
  1.5 0.0 copy-start
  1.5 1.4 %copy-done = bf16[1,6144,128]{2,1,0:T(8,128)(2,1)S(1)} copy-done((bf16[1,6144,128]{2,1,0:T(8,128)(2,1)S(1)}, bf16[1,6144,128]{2,1,0:T(8,128)(2,1)}, u32[]{:S(2)}) %copy-start) | copy-done | bytes 1572888
  2.9 0.0 copy-start.1
  3.0 1.4 %copy-done.1 = bf16[1,6144,128]{2,1,0:T(8,128)(2,1)S(1)} copy-done((bf16[1,6144,128]{2,1,0:T(8,128)(2,1)S(1)}, bf16[1,6144,128]{2,1,0:T(8,128)(2,1)}, u32[]{:S(2)}) %copy-start.1) | copy-done | bytes 1572888
  4.4 0.0 copy-start.2
  4.4 1.4 %copy-done.2 = bf16[1,6144,128]{2,1,0:T(8,128)(2,1)S(1)} copy-done((bf16[1,6144,128]{2,1,0:T(8,128)(2,1)S(1)}, bf16[1,6144,128]{2,1,0:T(8,128)(2,1)}, u32[]{:S(2)}) %copy-start.2) | copy-done | bytes 1572888
  5.8 0.0 copy-start.3
  5.8 0.9 %copy-done.3 = bf16[64,768]{1,0:T(8,128)(2,1)S(1)} copy-done((bf16[64,768]{1,0:T(8,128)(2,1)S(1)}, bf16[64,768]{1,0:T(8,128)(2,1)}, u32[]{:S(2)}) %copy-start.3) | copy-done | bytes 98328
  6.7 70.4 %experts.1 = bf16[64,768]{1,0:T(8,128)(2,1)S(1)} custom-call(bf16[64,768]{1,0:T(8,128)(2,1)S(1)} %copy-done.3, s32[64,8]{1,0:T(8,128)S(1)} %copy.7.ids, f32[64,8]{1,0:T(8,128)S(1)} %copy.8.rw, bf16[1,6144,128]{2,1,0:T(8,128)(2,1)S(1)} %copy-done, bf16[1,6144,128]{2,1,0:T(8,128)(2,1)S(1)} %copy-done.1, bf16[1,6144,128]{2,1,0:T(8,128)(2,1)S(1)} %copy-done.2), custom_call_target="tpu_custom_call" | custom-call | flops 603979776 | bytes 4718592 | tf_op jit(solution)/shard_map/experts/pallas_call | solution.py:251
  77.1 0.6 copy.10
Async XLA Ops:
  1.5 1.4 %copy-start = (bf16[1,6144,128]{2,1,0:T(8,128)(2,1)S(1)}, bf16[1,6144,128]{2,1,0:T(8,128)(2,1)}, u32[]{:S(2)}) copy-start(bf16[1,6144,128]{2,1,0:T(8,128)(2,1)} %wg_hbm.1) | copy-start | bytes 4718596
  2.9 1.4 %copy-start.1 = (bf16[1,6144,128]{2,1,0:T(8,128)(2,1)S(1)}, bf16[1,6144,128]{2,1,0:T(8,128)(2,1)}, u32[]{:S(2)}) copy-start(bf16[1,6144,128]{2,1,0:T(8,128)(2,1)} %wu_hbm.1) | copy-start | bytes 4718596
  4.4 1.4 %copy-start.2 = (bf16[1,6144,128]{2,1,0:T(8,128)(2,1)S(1)}, bf16[1,6144,128]{2,1,0:T(8,128)(2,1)}, u32[]{:S(2)}) copy-start(bf16[1,6144,128]{2,1,0:T(8,128)(2,1)} %wd_hbm.1) | copy-start | bytes 4718596
  5.8 0.9 %copy-start.3 = (bf16[64,768]{1,0:T(8,128)(2,1)S(1)}, bf16[64,768]{1,0:T(8,128)(2,1)}, u32[]{:S(2)}) copy-start(bf16[64,768]{1,0:T(8,128)(2,1)} %tok.1) | copy-start | bytes 294916

commit v2 on v0

v2 whole, which is shorter than its diff:
```python
import jax
import jax.numpy as jnp
from jax import lax
from jax.experimental import pallas as pl
from jax.experimental.pallas import tpu as pltpu
from jax.sharding import PartitionSpec as P

MESH = pl.DeviceIdType.MESH
BF16 = jnp.bfloat16
F32 = jnp.float32
Y, Z, X = 4, 16, 4
TOK, FEAT, FF = 64, 768, 128
CHIP = 2 * FF
Q = 2
NF = 1
FH = FEAT // 2
F = FH // NF
SLOTS = Y * Z * 2


def dot(a, b, dims=((1,), (0,))):
    return lax.dot_general(a, b, (dims, ((), ())), preferred_element_type=F32)


def iota(shape, dim):
    return lax.broadcasted_iota(jnp.int32, shape, dim)


def shr(a, n):
    return lax.shift_right_logical(a, n)


def wait_bytes(ref, sem):
    pltpu.make_async_copy(ref, ref, sem).wait()


def kernel(
    tok, ids, rw, wg_hbm, wu_hbm, wd_hbm, out,
    wgu, wd, ysend, yrecv, zsend, xall, part, other, rsend, rrecv, mine,
    zsend2, zrecv2, ysend2, yrecv2, mixed,
    w_sem, w_ssem, w_rsem, y_ssem, y_rsem, z_ssem, z_rsem, x_ssem, x_rsem, p_ssem, p_rsem,
    r_ssem, r_rsem, z2_ssem, z2_rsem, y2_ssem, y2_rsem,
):
    e, w = lax.axis_index("expert"), lax.axis_index("width")
    y, z = e // Z, e % Z
    x, core = w // 2, w % 2
    partner = x * 2 + (1 - core)
    xl, xr, xo = (x + X - 1) % X, (x + 1) % X, (x + 2) % X
    around = [xo, xr, xl]

    def ypeer(d):
        return (y + d) % Y

    def zpeer(d):
        return (z + d) % Z

    yorder = [2, 1, 3]
    zorder = [8, 7, 9, 6, 10, 5, 11, 4, 12, 3, 13, 2, 14, 1, 15]

    def columns(n):
        return pl.ds(pl.multiple_of(n * CHIP + core * FF, FF), FF)

    places = [(wg_hbm, wgu, 0), (wu_hbm, wgu, 1), (wd_hbm, wd, 0)]
    weights = [
        pltpu.make_async_copy(src.at[:, core], dst.at[:, :, columns(n)], w_sem.at[i])
        for i, (src, dst, n) in enumerate(places)
    ]

    bar = pltpu.get_barrier_semaphore()

    def greet(ee, ww):
        pl.semaphore_signal(bar, inc=1, device_id=(ee, ww), device_id_type=MESH)

    for d in zorder:
        greet(y * Z + zpeer(d), w)
    for d in yorder:
        greet(ypeer(d) * Z + z, w)
    for xx in around:
        greet(e, xx * 2 + core)
    greet(e, partner)
    for copy in weights:
        copy.start()

    def remote(src, dst, ssem, rsem, ee, ww):
        pltpu.make_async_remote_copy(
            src_ref=src, dst_ref=dst, send_sem=ssem, recv_sem=rsem,
            device_id=(ee, ww), device_id_type=MESH,
        ).start()

    row = iota((SLOTS, TOK), 0)
    expert = shr(row, 1)
    match = jnp.zeros((SLOTS, TOK), F32)
    weight = jnp.zeros((SLOTS, TOK), F32)
    for k in range(ids.shape[0]):
        hit = ids[k : k + 1, :] == expert
        match = jnp.where(hit, 1.0, match)
        weight = jnp.where(hit, rw[k : k + 1, :], weight)
    earlier = jnp.where(iota((TOK, TOK), 0) < iota((TOK, TOK), 1), 1.0, 0.0).astype(BF16)
    rank = dot(match.astype(BF16), earlier)
    chosen = [jnp.where(rank == float(q), match, 0.0) for q in range(Q)]
    half = [(row & 1) == h for h in range(2)]
    for q in range(Q):
        rows = sum(
            dot(jnp.where(half[h], chosen[q], 0.0).astype(BF16), tok[:, h * FH : (h + 1) * FH]) for h in range(2)
        ).astype(BF16)
        for f in range(NF):
            ysend[q, f] = rows[:, f * F : (f + 1) * F].reshape(Y, Z * 2, F)

    def order(a, b):
        return lax.shift_left(a & 3, 5) + lax.shift_left(shr(a, 3), 1) + (shr(a, 2) & 1) == b

    i0, i1 = iota((SLOTS, SLOTS), 0), iota((SLOTS, SLOTS), 1)
    to_z = jnp.where(order(i0, i1), 1.0, 0.0).astype(BF16)
    to_y = jnp.where(order(i1, i0), 1.0, 0.0).astype(BF16)
    first = (shr(iota((SLOTS, F), 0), 2) & 1) == 0

    pl.semaphore_wait(bar, len(zorder) + len(yorder) + len(around) + 1)

    def out_y(q, f):
        for d in yorder:
            remote(ysend.at[q, f, ypeer(d)], yrecv.at[q, f, y], y_ssem, y_rsem.at[q, f], ypeer(d) * Z + z, w)
        pltpu.make_async_copy(ysend.at[q, f, y], yrecv.at[q, f, y], y_rsem.at[q, f]).start()

    def trade_weights(q, f):
        for i, (src, dst, n) in enumerate(places):
            remote(src.at[:, 1 - core], dst.at[:, :, columns(n)], w_ssem.at[i], w_rsem.at[i], e, partner)

    def out_z(q, f):
        wait_bytes(yrecv.at[q, f], y_rsem.at[q, f])
        zsend[q, f] = dot(to_z, yrecv[q, f].reshape(SLOTS, F)).astype(BF16).reshape(Z, Y * 2, F)
        for d in zorder:
            remote(
                zsend.at[q, f, zpeer(d)], xall.at[q, f, x, z], z_ssem, z_rsem.at[q, f], y * Z + zpeer(d), w
            )
        pltpu.make_async_copy(zsend.at[q, f, z], xall.at[q, f, x, z], z_rsem.at[q, f]).start()

    def project(q, f, xx):
        block = xall[q, f, xx].reshape(SLOTS, F)
        low = jnp.where(first, block, jnp.zeros_like(block))
        high = jnp.where(first, jnp.zeros_like(block), block)
        return dot(low, wgu[xx, f * F : (f + 1) * F]) + dot(high, wgu[xx, FH + f * F : FH + (f + 1) * F])

    def out_x(q, f):
        wait_bytes(xall.at[q, f, x], z_rsem.at[q, f])
        for i, xx in enumerate(around):
            ref = xall.at[q, f, x]
            remote(ref, ref, x_ssem, x_rsem.at[q, f, i], e, xx * 2 + core)

    def weights_here(q, f):
        for copy in weights:
            copy.wait()
        for i, (src, dst, n) in enumerate(places):
            ref = dst.at[:, :, pl.ds(0, FF)]
            wait_bytes(ref, w_rsem.at[i])

    def gathered(q, f):
        total = project(q, f, x)
        for i, xx in ((1, xl), (2, xr), (0, xo)):
            wait_bytes(xall.at[q, f, xx], x_rsem.at[q, f, i])
            total = total + project(q, f, xx)
        if f > 0:
            total = total + part[q]
        part[q] = total
        if f == NF - 1:
            remote(part.at[q], other.at[q], p_ssem, p_rsem.at[q], e, partner)

    hidden = {}

    def activate(q, f):
        wait_bytes(other.at[q], p_rsem.at[q])
        total = part[q] + other[q]
        total = total.reshape(Z, Y * 2, 2 * CHIP)
        total = (total + pltpu.roll(total, Y, 1)).reshape(SLOTS, 2 * CHIP)
        gate, up = total[:, :CHIP], total[:, CHIP:]
        hidden[q] = (gate / (1.0 + jnp.exp(-gate)) * up).astype(BF16)

    def down(q, f, xx):
        low = dot(hidden[q], wd[xx, f * F : (f + 1) * F], ((1,), (1,)))
        high = dot(hidden[q], wd[xx, FH + f * F : FH + (f + 1) * F], ((1,), (1,)))
        return jnp.where(first, low, high)

    def back_x(q, f):
        for i, xx in enumerate(around):
            rsend[q, f, i] = down(q, f, xx).astype(BF16)
            remote(rsend.at[q, f, i], rrecv.at[q, f, i], r_ssem, r_rsem.at[q, f, i], e, xx * 2 + core)
        mine[q, f] = down(q, f, x)

    def back_z(q, f):
        total = mine[q, f]
        for i in (1, 2, 0):
            wait_bytes(rrecv.at[q, f, i], r_rsem.at[q, f, i])
            total = total + rrecv[q, f, i].astype(F32)
        zsend2[q, f] = total.astype(BF16).reshape(Z, Y * 2, F)
        for d in zorder:
            remote(
                zsend2.at[q, f, zpeer(d)], zrecv2.at[q, f, z], z2_ssem, z2_rsem.at[q, f], y * Z + zpeer(d), w
            )
        pltpu.make_async_copy(zsend2.at[q, f, z], zrecv2.at[q, f, z], z2_rsem.at[q, f]).start()

    def back_y(q, f):
        wait_bytes(zrecv2.at[q, f], z2_rsem.at[q, f])
        rows = dot(to_y, zrecv2[q, f].reshape(SLOTS, F)).astype(BF16)
        ysend2[q, f] = rows.reshape(Y, Z * 2, F)
        for d in yorder:
            remote(
                ysend2.at[q, f, ypeer(d)], yrecv2.at[q, f, y], y2_ssem, y2_rsem.at[q, f], ypeer(d) * Z + z, w
            )
        pltpu.make_async_copy(ysend2.at[q, f, y], yrecv2.at[q, f, y], y2_rsem.at[q, f]).start()

    def combine(q, f):
        wait_bytes(yrecv2.at[q, f], y2_rsem.at[q, f])
        returned = yrecv2[q, f].reshape(SLOTS, F)
        for h in range(2):
            coeff = jnp.where(half[h], weight * chosen[q], 0.0)
            high = coeff.astype(BF16)
            low = (coeff - high.astype(F32)).astype(BF16)
            total = dot(high, returned, ((0,), (0,))) + dot(low, returned, ((0,), (0,)))
            place = slice(h * FH + f * F, h * FH + (f + 1) * F)
            if q > 0:
                total = total + mixed[:, place]
            if q < Q - 1:
                mixed[:, place] = total
            else:
                out[:, place] = total.astype(BF16)

    gap = 3.5 / NF
    ready = 19.0 + gap * (NF - 1)
    steps = [
        (out_y, 0.0, 0.1, NF), (trade_weights, 0.3, 0, 0), (out_z, 2.6, 0.5, NF), (out_x, 9.0, gap, NF),
        (weights_here, 9.1, 0, 0), (gathered, 16.0, gap, NF), (activate, ready, gap * NF, 1),
        (back_x, ready + 0.1, gap, NF), (back_z, ready + 7.0, gap, NF), (back_y, ready + 13.0, gap, NF),
        (combine, ready + 16.0, gap, NF),
    ]
    plan = []
    for s, (step, at, later, each) in enumerate(steps):
        for q in range(Q if each else 1):
            for f in range(each or 1):
                plan.append((at + later * (q * each + f), s, q, f))
    for _, s, q, f in sorted(plan):
        steps[s][0](q, f)

    for i, (src, dst, n) in enumerate(places):
        wait_bytes(src.at[:, 1 - core], w_ssem.at[i])
    wait_bytes(ysend.at[:, :, pl.ds(0, Y - 1)], y_ssem)
    wait_bytes(zsend.at[:, :, pl.ds(0, Z - 1)], z_ssem)
    wait_bytes(xall.at[:, :, pl.ds(0, X - 1)], x_ssem)
    wait_bytes(part, p_ssem)
    wait_bytes(rsend, r_ssem)
    wait_bytes(zsend2.at[:, :, pl.ds(0, Z - 1)], z2_ssem)
    wait_bytes(ysend2.at[:, :, pl.ds(0, Y - 1)], y2_ssem)


def body(tokens, expert_ids, route_weight, gate_weight, up_weight, down_weight):
    vmem = pl.BlockSpec(memory_space=pltpu.VMEM)
    hbm = pl.BlockSpec(memory_space=pl.ANY)
    dma = pltpu.SemaphoreType.DMA
    ystage, zstage = pltpu.VMEM((Q, NF, Y, Z * 2, F), BF16), pltpu.VMEM((Q, NF, Z, Y * 2, F), BF16)
    return pl.pallas_call(
        kernel,
        out_shape=jax.ShapeDtypeStruct((TOK, FEAT), BF16),
        in_specs=[vmem, vmem, vmem, hbm, hbm, hbm],
        out_specs=vmem,
        scratch_shapes=[
            pltpu.VMEM((X, FEAT, 2 * CHIP), BF16),
            pltpu.VMEM((X, FEAT, CHIP), BF16),
            ystage, ystage, zstage,
            pltpu.VMEM((Q, NF, X, Z, Y * 2, F), BF16),
            pltpu.VMEM((Q, SLOTS, 2 * CHIP), F32),
            pltpu.VMEM((Q, SLOTS, 2 * CHIP), F32),
            pltpu.VMEM((Q, NF, X - 1, SLOTS, F), BF16),
            pltpu.VMEM((Q, NF, X - 1, SLOTS, F), BF16),
            pltpu.VMEM((Q, NF, SLOTS, F), F32),
            zstage, zstage, ystage, ystage,
            pltpu.VMEM((TOK, FEAT), F32),
            dma((3,)), dma((3,)), dma((3,)),
            dma, dma((Q, NF)), dma, dma((Q, NF)), dma, dma((Q, NF, X - 1)), dma, dma((Q,)),
            dma, dma((Q, NF, X - 1)), dma, dma((Q, NF)), dma, dma((Q, NF)),
        ],
        compiler_params=pltpu.CompilerParams(
            collective_id=0, has_side_effects=True, vmem_limit_bytes=60 * 2**20
        ),
        cost_estimate=pl.CostEstimate(
            flops=12 * SLOTS * X * 2 * FEAT * FF, bytes_accessed=12 * X * FEAT * FF, transcendentals=SLOTS * CHIP
        ),
        name="experts",
    )(
        tokens, expert_ids.T, route_weight.T,
        *(a.reshape(X, 2, FEAT, FF) for a in (gate_weight, up_weight, down_weight)),
    )


def solution(mesh):
    in_specs = (
        P("expert", "width"),
        P("expert", None),
        P("expert", None),
        P("expert", None, "width"),
        P("expert", None, "width"),
        P("expert", None, "width"),
    )
    out_specs = P("expert", "width")
    return jax.shard_map(body, mesh=mesh, in_specs=in_specs, out_specs=out_specs, check_vma=False)
```

time: 138 us -> 63 us (0.46)
  blocking collectives: 86.9 us -> 0 us
  Pallas kernels: 0 us -> 61.3 us
  local copies, waits for them, and re-layouts: 20.5 us -> 1.54 us
  waiting for transfers between devices: 17.4 us -> 0 us
  starting transfers between devices: 6.57 us -> 0 us
  matrix products: 5.24 us -> 0 us
    all_to_all x3 -> x0, blocking collectives: 86.9 us -> none  [the longest x1 36.6 us: body(): lax.all_to_all(outgoing.reshape(holders, SEND, outgoing.shape[1]), 'exper...]
    pallas_call x0 -> x1, Pallas kernels: none -> 61.3 us  [body(): pl.pallas_call(kernel, out_shape=jax.ShapeDtypeStruct((TOK, FEAT), BF16),...]
    all_to_all x1 -> x0, waiting for transfers between devices: 17.4 us -> none  [body(): lax.all_to_all(summed.reshape(feature_rows, holders, SEND).astype(jnp.bfl...]
    scatter x1 -> x0, local copies, waits for them, and re-layouts: 15.5 us -> none  [body(): slot_table = jnp.full((capacity + 1,), tok_rows, jnp.int32).at[slot_of.re...]
    all_to_all x1 -> x0, starting transfers between devices: 6.57 us -> none  [body(): lax.all_to_all(summed.reshape(feature_rows, holders, SEND).astype(jnp.bfl...]
    dot_general x3 -> x0, matrix products: 5.24 us -> none  [the longest x1 3.69 us: body(): lax.dot_general(down_mat, hidden, (((1,), (1,)), ((), ())), preferred_ele...]
    reshape x4 -> x0, local copies, waits for them, and re-layouts: 1.82 us -> none  [the longest x1 1.51 us: cut_along(): parts = array.reshape(*dims[:dim], size, dims[dim] // size, *dims[dim + 1:])]
  transfers between devices with their start and end apart: 1 -> 0, of which waited for: 1 -> 0; matrix products, arithmetic and copies ran while one was open for 0% -> 0% of each run, Pallas kernels for 0% -> 0%
where the time goes in v2:
time: 63 us; the launch traced here: 62.9 us
  Pallas kernels  61.3 us (97%)
  local copies, waits for them, and re-layouts  1.54 us (2%)
    pallas_call x1, Pallas kernels, body(): pl.pallas_call(kernel, out_shape=jax.ShapeDtypeStruct((TOK, FEAT), BF16),...  61.3 us
    unnamed x1, local copies, waits for them, and re-layouts  1.54 us

profile of v2, /device:TPU:8, one launch (start us, length us, event | category | flops | bytes accessed | tf_op | source)
XLA Modules:
  0.0 62.9 jit_solution(6594970324128978500)
XLA Ops:
  0.0 61.3 %experts.1 = bf16[64,768]{1,0:T(8,128)(2,1)} custom-call(bf16[64,768]{1,0:T(8,128)(2,1)} %tok.1, s32[8,64]{1,0:T(8,128)} %bitcast.8, f32[8,64]{1,0:T(8,128)} %bitcast.9, bf16[4,2,768,128]{3,2,1,0:T(8,128)(2,1)} %bitcast.5, bf16[4,2,768,128]{3,2,1,0:T(8,128)(2,1)} %bitcast.6, bf16[4,2,768,128]{3,2,1,0:T(8,128)(2,1)} %bitcast.7), custom_call_target="tpu_custom_call" | custom-call | flops 1207959552 | bytes 4718592 | tf_op jit(solution)/shard_map/experts/pallas_call | solution.py:258
  61.3 1.5 %copy.8 = bf16[64,768]{1,0:T(8,128)(2,1)} copy(bf16[64,768]{1,0:T(8,128)(2,1)} %experts.1) | data formatting | bytes 196608

commit v3 on v2

--- a/solution.py
+++ b/solution.py
@@ -12,9 +12,12 @@
 TOK, FEAT, FF = 64, 768, 128
 CHIP = 2 * FF
 Q = 2
+TW = 0.3
 NF = 1
 FH = FEAT // 2
 F = FH // NF
+LANES = 128
+TILES = FEAT // LANES
 SLOTS = Y * Z * 2
 
 
@@ -37,9 +40,9 @@
 def kernel(
     tok, ids, rw, wg_hbm, wu_hbm, wd_hbm, out,
     wgu, wd, ysend, yrecv, zsend, xall, part, other, rsend, rrecv, mine,
-    zsend2, zrecv2, ysend2, yrecv2, mixed,
+    rows_zh, rows_ej, dsend, drecv, mixed,
     w_sem, w_ssem, w_rsem, y_ssem, y_rsem, z_ssem, z_rsem, x_ssem, x_rsem, p_ssem, p_rsem,
-    r_ssem, r_rsem, z2_ssem, z2_rsem, y2_ssem, y2_rsem,
+    r_ssem, r_rsem, d_ssem, d_rsem,
 ):
     e, w = lax.axis_index("expert"), lax.axis_index("width")
     y, z = e // Z, e % Z
@@ -78,26 +81,26 @@
     for xx in around:
         greet(e, xx * 2 + core)
     greet(e, partner)
-    for copy in weights:
-        copy.start()
-
     def remote(src, dst, ssem, rsem, ee, ww):
         pltpu.make_async_remote_copy(
             src_ref=src, dst_ref=dst, send_sem=ssem, recv_sem=rsem,
             device_id=(ee, ww), device_id_type=MESH,
         ).start()
 
+    earlier = jnp.where(iota((TOK, TOK), 0) < iota((TOK, TOK), 1), 1.0, 0.0).astype(BF16)
+
+    def routed(expert):
+        match = jnp.zeros(expert.shape, F32)
+        weight = jnp.zeros(expert.shape, F32)
+        for k in range(ids.shape[0]):
+            hit = ids[k : k + 1, :] == expert
+            match = jnp.where(hit, 1.0, match)
+            weight = jnp.where(hit, rw[k : k + 1, :], weight)
+        rank = dot(match.astype(BF16), earlier)
+        return [jnp.where(rank == float(q), match, 0.0) for q in range(Q)], weight
+
     row = iota((SLOTS, TOK), 0)
-    expert = shr(row, 1)
-    match = jnp.zeros((SLOTS, TOK), F32)
-    weight = jnp.zeros((SLOTS, TOK), F32)
-    for k in range(ids.shape[0]):
-        hit = ids[k : k + 1, :] == expert
-        match = jnp.where(hit, 1.0, match)
-        weight = jnp.where(hit, rw[k : k + 1, :], weight)
-    earlier = jnp.where(iota((TOK, TOK), 0) < iota((TOK, TOK), 1), 1.0, 0.0).astype(BF16)
-    rank = dot(match.astype(BF16), earlier)
-    chosen = [jnp.where(rank == float(q), match, 0.0) for q in range(Q)]
+    chosen, _ = routed(shr(row, 1))
     half = [(row & 1) == h for h in range(2)]
     for q in range(Q):
         rows = sum(
@@ -106,12 +109,17 @@
         for f in range(NF):
             ysend[q, f] = rows[:, f * F : (f + 1) * F].reshape(Y, Z * 2, F)
 
+    coeffs = []
+    ones, weight = routed(iota((Y * Z, TOK), 0))
+    for q in range(Q):
+        high = (weight * ones[q]).astype(BF16)
+        coeffs.append((high, (weight * ones[q] - high.astype(F32)).astype(BF16)))
+
     def order(a, b):
         return lax.shift_left(a & 3, 5) + lax.shift_left(shr(a, 3), 1) + (shr(a, 2) & 1) == b
 
     i0, i1 = iota((SLOTS, SLOTS), 0), iota((SLOTS, SLOTS), 1)
     to_z = jnp.where(order(i0, i1), 1.0, 0.0).astype(BF16)
-    to_y = jnp.where(order(i1, i0), 1.0, 0.0).astype(BF16)
     first = (shr(iota((SLOTS, F), 0), 2) & 1) == 0
 
     pl.semaphore_wait(bar, len(zorder) + len(yorder) + len(around) + 1)
@@ -122,6 +130,8 @@
         pltpu.make_async_copy(ysend.at[q, f, y], yrecv.at[q, f, y], y_rsem.at[q, f]).start()
 
     def trade_weights(q, f):
+        for copy in weights:
+            copy.start()
         for i, (src, dst, n) in enumerate(places):
             remote(src.at[:, 1 - core], dst.at[:, :, columns(n)], w_ssem.at[i], w_rsem.at[i], e, partner)
 
@@ -185,51 +195,47 @@
             remote(rsend.at[q, f, i], rrecv.at[q, f, i], r_ssem, r_rsem.at[q, f, i], e, xx * 2 + core)
         mine[q, f] = down(q, f, x)
 
-    def back_z(q, f):
+    def back(q, f):
         total = mine[q, f]
         for i in (1, 2, 0):
             wait_bytes(rrecv.at[q, f, i], r_rsem.at[q, f, i])
             total = total + rrecv[q, f, i].astype(F32)
-        zsend2[q, f] = total.astype(BF16).reshape(Z, Y * 2, F)
-        for d in zorder:
-            remote(
-                zsend2.at[q, f, zpeer(d)], zrecv2.at[q, f, z], z2_ssem, z2_rsem.at[q, f], y * Z + zpeer(d), w
-            )
-        pltpu.make_async_copy(zsend2.at[q, f, z], zrecv2.at[q, f, z], z2_rsem.at[q, f]).start()
-
-    def back_y(q, f):
-        wait_bytes(zrecv2.at[q, f], z2_rsem.at[q, f])
-        rows = dot(to_y, zrecv2[q, f].reshape(SLOTS, F)).astype(BF16)
-        ysend2[q, f] = rows.reshape(Y, Z * 2, F)
-        for d in yorder:
-            remote(
-                ysend2.at[q, f, ypeer(d)], yrecv2.at[q, f, y], y2_ssem, y2_rsem.at[q, f], ypeer(d) * Z + z, w
-            )
-        pltpu.make_async_copy(ysend2.at[q, f, y], yrecv2.at[q, f, y], y2_rsem.at[q, f]).start()
+        for c in range(TILES // 2):
+            rows_zh[pl.ds(c * SLOTS, SLOTS), :] = total[:, c * LANES : (c + 1) * LANES]
+        for h in range(2):
+            for yy in range(Y):
+                for c in range(TILES // 2):
+                    rows_ej[pl.ds(yy * Z * TILES + h * TILES // 2 + c, Z, TILES), :] = rows_zh[
+                        pl.ds(c * SLOTS + h * Y + yy, Z, 2 * Y), :
+                    ]
+        dsend[q] = rows_ej[...].astype(BF16).reshape(Y * Z, TILES // 2, 2, LANES)
+        for d in zorder + [0]:
+            for dy in yorder + [0]:
+                if d or dy:
+                    peer = ypeer(dy) * Z + zpeer(d)
+                    remote(dsend.at[q, peer], drecv.at[q, e], d_ssem, d_rsem.at[q], peer, w)
+        pltpu.make_async_copy(dsend.at[q, e], drecv.at[q, e], d_rsem.at[q]).start()
 
     def combine(q, f):
-        wait_bytes(yrecv2.at[q, f], y2_rsem.at[q, f])
-        returned = yrecv2[q, f].reshape(SLOTS, F)
-        for h in range(2):
-            coeff = jnp.where(half[h], weight * chosen[q], 0.0)
-            high = coeff.astype(BF16)
-            low = (coeff - high.astype(F32)).astype(BF16)
-            total = dot(high, returned, ((0,), (0,))) + dot(low, returned, ((0,), (0,)))
-            place = slice(h * FH + f * F, h * FH + (f + 1) * F)
-            if q > 0:
-                total = total + mixed[:, place]
-            if q < Q - 1:
-                mixed[:, place] = total
-            else:
-                out[:, place] = total.astype(BF16)
+        wait_bytes(drecv.at[q], d_rsem.at[q])
+        rows_ej[...] = drecv[q].astype(F32).reshape(Y * Z * TILES, LANES)
+        returned = jnp.concatenate(
+            [rows_ej[pl.ds(j, Y * Z, TILES), :].astype(BF16) for j in range(TILES)], axis=1
+        )
+        total = sum(dot(c, returned, ((0,), (0,))) for c in coeffs[q])
+        if q > 0:
+            total = total + mixed[...]
+        if q < Q - 1:
+            mixed[...] = total
+        else:
+            out[...] = total.astype(BF16)
 
     gap = 3.5 / NF
     ready = 19.0 + gap * (NF - 1)
     steps = [
-        (out_y, 0.0, 0.1, NF), (trade_weights, 0.3, 0, 0), (out_z, 2.6, 0.5, NF), (out_x, 9.0, gap, NF),
+        (out_y, 0.0, 0.1, NF), (trade_weights, TW, 0, 0), (out_z, 2.6, 0.5, NF), (out_x, 9.0, gap, NF),
         (weights_here, 9.1, 0, 0), (gathered, 16.0, gap, NF), (activate, ready, gap * NF, 1),
-        (back_x, ready + 0.1, gap, NF), (back_z, ready + 7.0, gap, NF), (back_y, ready + 13.0, gap, NF),
-        (combine, ready + 16.0, gap, NF),
+        (back_x, ready + 0.1, gap, NF), (back, ready + 7.0, gap, NF), (combine, ready + 15.0, gap, NF),
     ]
     plan = []
     for s, (step, at, later, each) in enumerate(steps):
@@ -246,8 +252,7 @@
     wait_bytes(xall.at[:, :, pl.ds(0, X - 1)], x_ssem)
     wait_bytes(part, p_ssem)
     wait_bytes(rsend, r_ssem)
-    wait_bytes(zsend2.at[:, :, pl.ds(0, Z - 1)], z2_ssem)
-    wait_bytes(ysend2.at[:, :, pl.ds(0, Y - 1)], y2_ssem)
+    wait_bytes(dsend.at[:, pl.ds(0, Y * Z - 1)], d_ssem)
 
 
 def body(tokens, expert_ids, route_weight, gate_weight, up_weight, down_weight):
@@ -270,11 +275,14 @@
             pltpu.VMEM((Q, NF, X - 1, SLOTS, F), BF16),
             pltpu.VMEM((Q, NF, X - 1, SLOTS, F), BF16),
             pltpu.VMEM((Q, NF, SLOTS, F), F32),
-            zstage, zstage, ystage, ystage,
+            pltpu.VMEM((TILES // 2 * SLOTS, LANES), F32),
+            pltpu.VMEM((Y * Z * TILES, LANES), F32),
+            pltpu.VMEM((Q, Y * Z, TILES // 2, 2, LANES), BF16),
+            pltpu.VMEM((Q, Y * Z, TILES // 2, 2, LANES), BF16),
             pltpu.VMEM((TOK, FEAT), F32),
             dma((3,)), dma((3,)), dma((3,)),
             dma, dma((Q, NF)), dma, dma((Q, NF)), dma, dma((Q, NF, X - 1)), dma, dma((Q,)),
-            dma, dma((Q, NF, X - 1)), dma, dma((Q, NF)), dma, dma((Q, NF)),
+            dma, dma((Q, NF, X - 1)), dma, dma((Q,)),
         ],
         compiler_params=pltpu.CompilerParams(
             collective_id=0, has_side_effects=True, vmem_limit_bytes=60 * 2**20

time: 63 us -> 60.3 us (0.957)
  the two profiles are of different devices: /device:TPU:8 before, /device:TPU:2 now
where the time goes in v3:
time: 60.3 us; the launch traced here: 60.1 us
  Pallas kernels  58.6 us (97%)
  local copies, waits for them, and re-layouts  1.54 us (3%)
    pallas_call x1, Pallas kernels, body(): pl.pallas_call(kernel, out_shape=jax.ShapeDtypeStruct((TOK, FEAT), BF16),...  58.6 us
    unnamed x1, local copies, waits for them, and re-layouts  1.54 us

profile of v3, /device:TPU:2, one launch (start us, length us, event | category | flops | bytes accessed | tf_op | source)
XLA Modules:
  0.0 60.1 jit_solution(8374586330389037706)
XLA Ops:
  0.0 58.6 %experts.1 = bf16[64,768]{1,0:T(8,128)(2,1)} custom-call(bf16[64,768]{1,0:T(8,128)(2,1)} %tok.1, s32[8,64]{1,0:T(8,128)} %bitcast.8, f32[8,64]{1,0:T(8,128)} %bitcast.9, bf16[4,2,768,128]{3,2,1,0:T(8,128)(2,1)} %bitcast.5, bf16[4,2,768,128]{3,2,1,0:T(8,128)(2,1)} %bitcast.6, bf16[4,2,768,128]{3,2,1,0:T(8,128)(2,1)} %bitcast.7), custom_call_target="tpu_custom_call" | custom-call | flops 1207959552 | bytes 4718592 | tf_op jit(solution)/shard_map/experts/pallas_call | solution.py:263
  58.6 1.5 %copy.8 = bf16[64,768]{1,0:T(8,128)(2,1)} copy(bf16[64,768]{1,0:T(8,128)(2,1)} %experts.1) | data formatting | bytes 196608

commit v4 on v3

v4 whole, which is shorter than its diff:
```python
import jax
import jax.numpy as jnp
from jax import lax
from jax.experimental import pallas as pl
from jax.experimental.pallas import tpu as pltpu
from jax.sharding import PartitionSpec as P

MESH = pl.DeviceIdType.MESH
BF16 = jnp.bfloat16
F32 = jnp.float32
Y, Z, X = 4, 16, 4
TOK, FEAT, FF = 64, 768, 128
CHIP = 2 * FF
Q = 2
ALL = Y * Z
K = Q * 2
ROWS = ALL // 2
LANES = 128
TILES = FEAT // LANES


def dot(a, b, dims=((1,), (0,))):
    return lax.dot_general(a, b, (dims, ((), ())), preferred_element_type=F32)


def iota(shape, dim):
    return lax.broadcasted_iota(jnp.int32, shape, dim)


def wait_bytes(ref, sem):
    pltpu.make_async_copy(ref, ref, sem).wait()


def kernel(
    tok, ids, rw, wg_hbm, wu_hbm, wd_hbm, out,
    wgu, wd, flat, osend, orecv, xall, part, other, rsend, rrecv, mine, dsend, drecv, mixed,
    w_sem, w_ssem, w_rsem, column_sem, o_ssem, o_rsem, x_ssem, x_rsem, p_ssem, p_rsem,
    r_ssem, r_rsem, d_ssem, d_rsem,
):
    e, w = lax.axis_index("expert"), lax.axis_index("width")
    y, z = e // Z, e % Z
    x, core = w // 2, w % 2
    partner = x * 2 + (1 - core)
    xl, xr, xo = (x + X - 1) % X, (x + 1) % X, (x + 2) % X
    around = [xo, xr, xl]
    yorder = [2, 1, 3]
    zorder = [8, 7, 9, 6, 10, 5, 11, 4, 12, 3, 13, 2, 14, 1, 15]

    def peer(dy, dz):
        return (y + dy) % Y * Z + (z + dz) % Z

    near = [(0, dz) for dz in zorder] + [(dy, 0) for dy in yorder]
    far = [(dy, dz) for dz in zorder for dy in yorder]

    def place(ee):
        return ee // 2

    def parity(peers, p):
        return [(dy, dz) for dy, dz in peers if dz % 2 == p]

    def columns(n):
        return pl.ds(pl.multiple_of(n * CHIP + core * FF, FF), FF)

    places = [(wg_hbm, wgu, 0), (wu_hbm, wgu, 1), (wd_hbm, wd, 0)]
    weights = [
        pltpu.make_async_copy(src.at[:, core], dst.at[:, :, columns(n)], w_sem.at[i])
        for i, (src, dst, n) in enumerate(places)
    ]

    bar = pltpu.get_barrier_semaphore()

    def greet(ee, ww):
        pl.semaphore_signal(bar, inc=1, device_id=(ee, ww), device_id_type=MESH)

    for dy, dz in near:
        greet(peer(dy, dz), w)
    for xx in around:
        greet(e, xx * 2 + core)
    greet(e, partner)

    def remote(src, dst, ssem, rsem, ee, ww):
        pltpu.make_async_remote_copy(
            src_ref=src, dst_ref=dst, send_sem=ssem, recv_sem=rsem,
            device_id=(ee, ww), device_id_type=MESH,
        ).start()

    def fold(rows):
        n = rows.shape[0]
        for j in range(TILES):
            flat[pl.ds(j, n, TILES), :] = rows[:, j * LANES : (j + 1) * LANES]
        return flat[pl.ds(0, n * TILES), :].astype(BF16).reshape(n, TILES // 2, 2, LANES)

    def unfold(rows):
        n = rows.shape[0]
        flat[pl.ds(0, n * TILES), :] = rows.astype(F32).reshape(n * TILES, LANES)
        return jnp.concatenate([flat[pl.ds(j, n, TILES), :].astype(BF16) for j in range(TILES)], axis=1)

    expert = iota((ALL, TOK), 0)
    match = jnp.zeros((ALL, TOK), F32)
    weight = jnp.zeros((ALL, TOK), F32)
    for k in range(ids.shape[0]):
        hit = ids[k : k + 1, :] == expert
        match = jnp.where(hit, 1.0, match)
        weight = jnp.where(hit, rw[k : k + 1, :], weight)
    earlier = jnp.where(iota((TOK, TOK), 0) < iota((TOK, TOK), 1), 1.0, 0.0).astype(BF16)
    rank = dot(match.astype(BF16), earlier)
    coeffs = []
    for q in range(Q):
        chosen = jnp.where(rank == float(q), match, 0.0)
        high = (weight * chosen).astype(BF16)
        coeffs.append((high, (weight * chosen - high.astype(F32)).astype(BF16)))
        osend[q] = fold(dot(chosen.astype(BF16), tok[...]))

    pl.semaphore_wait(bar, len(near) + len(around) + 1)

    def column_is_in():
        for dy in yorder:
            pl.semaphore_signal(column_sem, inc=1, device_id=(peer(dy, 0), w), device_id_type=MESH)

    def columns_are_in():
        pl.semaphore_wait(column_sem, len(yorder))

    def out_to(k, peers):
        q, p = k // 2, k % 2
        for dy, dz in parity(peers, p):
            remote(
                osend.at[q, peer(dy, dz)], orecv.at[k, place(e)], o_ssem, o_rsem.at[k], peer(dy, dz), w
            )

    def out_own(q):
        pltpu.make_async_copy(osend.at[q, e], orecv.at[q * 2, place(e)], o_rsem.at[q * 2]).start()

    def start_weights():
        for copy in weights:
            copy.start()
        for i, (src, dst, n) in enumerate(places):
            remote(src.at[:, 1 - core], dst.at[:, :, columns(n)], w_ssem.at[i], w_rsem.at[i], e, partner)

    def weights_here():
        for copy in weights:
            copy.wait()
        for i, (src, dst, n) in enumerate(places):
            wait_bytes(dst.at[:, :, pl.ds(0, FF)], w_rsem.at[i])

    def out_x(k):
        wait_bytes(orecv.at[k], o_rsem.at[k])
        xall[k, x] = unfold(orecv[k])
        ref = xall.at[k, x]
        for i, xx in enumerate(around):
            remote(ref, ref, x_ssem, x_rsem.at[k, i], e, xx * 2 + core)

    def project(k, xx):
        return dot(xall[k, xx], wgu[xx])

    def gathered(k):
        total = project(k, x)
        for i, xx in ((1, xl), (2, xr), (0, xo)):
            wait_bytes(xall.at[k, xx], x_rsem.at[k, i])
            total = total + project(k, xx)
        part[k] = total
        remote(part.at[k], other.at[k], p_ssem, p_rsem.at[k], e, partner)

    def back_x(k):
        wait_bytes(other.at[k], p_rsem.at[k])
        total = part[k] + other[k]
        gate, up = total[:, :CHIP], total[:, CHIP:]
        hidden = (gate / (1.0 + jnp.exp(-gate)) * up).astype(BF16)
        for i, xx in enumerate(around):
            rsend[k, i] = dot(hidden, wd[xx], ((1,), (1,))).astype(BF16)
            remote(rsend.at[k, i], rrecv.at[k, i], r_ssem, r_rsem.at[k, i], e, xx * 2 + core)
        mine[k] = dot(hidden, wd[x], ((1,), (1,)))

    def back(k):
        total = mine[k]
        for i in (1, 2, 0):
            wait_bytes(rrecv.at[k, i], r_rsem.at[k, i])
            total = total + rrecv[k, i].astype(F32)
        dsend[k] = fold(total)
        q, p = k // 2, k % 2
        for dy, dz in parity(far, p) + parity(near, p):
            to = peer(dy, dz)
            remote(dsend.at[k, place(to)], drecv.at[q, e], d_ssem, d_rsem.at[q], to, w)
        if p == 0:
            pltpu.make_async_copy(dsend.at[k, place(e)], drecv.at[q, e], d_rsem.at[q]).start()

    def combine(q):
        wait_bytes(drecv.at[q], d_rsem.at[q])
        returned = unfold(drecv[q])
        total = sum(dot(c, returned, ((0,), (0,))) for c in coeffs[q])
        if q > 0:
            total = total + mixed[...]
        if q < Q - 1:
            mixed[...] = total
        else:
            out[...] = total.astype(BF16)

    column_is_in()
    for k in range(K):
        out_to(k, near)
    columns_are_in()
    for k in range(K):
        out_to(k, far)
        if k % 2 == 0:
            out_own(k // 2)
    start_weights()
    for k in range(K):
        out_x(k)
    weights_here()
    gathered(0)
    for k in range(1, K):
        gathered(k)
        back_x(k - 1)
    back_x(K - 1)
    for k in range(K):
        back(k)
    for q in range(Q):
        combine(q)

    for i, (src, dst, n) in enumerate(places):
        wait_bytes(src.at[:, 1 - core], w_ssem.at[i])
    wait_bytes(osend.at[:, pl.ds(0, ALL - 1)], o_ssem)
    wait_bytes(xall.at[:, pl.ds(0, X - 1)], x_ssem)
    wait_bytes(part, p_ssem)
    wait_bytes(rsend, r_ssem)
    wait_bytes(drecv.at[:, pl.ds(0, ALL - 1)], d_ssem)


def body(tokens, expert_ids, route_weight, gate_weight, up_weight, down_weight):
    vmem = pl.BlockSpec(memory_space=pltpu.VMEM)
    hbm = pl.BlockSpec(memory_space=pl.ANY)
    dma = pltpu.SemaphoreType.DMA
    lying = (TILES // 2, 2, LANES)
    return pl.pallas_call(
        kernel,
        out_shape=jax.ShapeDtypeStruct((TOK, FEAT), BF16),
        in_specs=[vmem, vmem, vmem, hbm, hbm, hbm],
        out_specs=vmem,
        scratch_shapes=[
            pltpu.VMEM((X, FEAT, 2 * CHIP), BF16),
            pltpu.VMEM((X, FEAT, CHIP), BF16),
            pltpu.VMEM((ALL * TILES, LANES), F32),
            pltpu.VMEM((Q, ALL, *lying), BF16),
            pltpu.VMEM((K, ROWS, *lying), BF16),
            pltpu.VMEM((K, X, ROWS, FEAT), BF16),
            pltpu.VMEM((K, ROWS, 2 * CHIP), F32),
            pltpu.VMEM((K, ROWS, 2 * CHIP), F32),
            pltpu.VMEM((K, X - 1, ROWS, FEAT), BF16),
            pltpu.VMEM((K, X - 1, ROWS, FEAT), BF16),
            pltpu.VMEM((K, ROWS, FEAT), F32),
            pltpu.VMEM((K, ROWS, *lying), BF16),
            pltpu.VMEM((Q, ALL, *lying), BF16),
            pltpu.VMEM((TOK, FEAT), F32),
            dma((3,)), dma((3,)), dma((3,)), pltpu.SemaphoreType.REGULAR,
            dma, dma((K,)), dma, dma((K, X - 1)), dma, dma((K,)),
            dma, dma((K, X - 1)), dma, dma((Q,)),
        ],
        compiler_params=pltpu.CompilerParams(
            collective_id=0, has_side_effects=True, vmem_limit_bytes=60 * 2**20
        ),
        cost_estimate=pl.CostEstimate(
            flops=12 * ALL * X * 2 * FEAT * FF, bytes_accessed=12 * X * FEAT * FF, transcendentals=2 * ALL * CHIP
        ),
        name="experts",
    )(
        tokens, expert_ids.T, route_weight.T,
        *(a.reshape(X, 2, FEAT, FF) for a in (gate_weight, up_weight, down_weight)),
    )


def solution(mesh):
    in_specs = (
        P("expert", "width"),
        P("expert", None),
        P("expert", None),
        P("expert", None, "width"),
        P("expert", None, "width"),
        P("expert", None, "width"),
    )
    out_specs = P("expert", "width")
    return jax.shard_map(body, mesh=mesh, in_specs=in_specs, out_specs=out_specs, check_vma=False)
```

time: 60.3 us -> 58.4 us (0.968)
  the two profiles are of different devices: /device:TPU:2 before, /device:TPU:33 now
where the time goes in v4:
time: 58.4 us; the launch traced here: 58.2 us
  Pallas kernels  56.7 us (97%)
  local copies, waits for them, and re-layouts  1.54 us (3%)
    pallas_call x1, Pallas kernels, body(): pl.pallas_call(kernel, out_shape=jax.ShapeDtypeStruct((TOK, FEAT), BF16),...  56.7 us
    unnamed x1, local copies, waits for them, and re-layouts  1.54 us

profile of v4, /device:TPU:33, one launch (start us, length us, event | category | flops | bytes accessed | tf_op | source)
XLA Modules:
  0.0 58.2 jit_solution(5847455733051896569)
XLA Ops:
  0.0 56.7 %experts.1 = bf16[64,768]{1,0:T(8,128)(2,1)} custom-call(bf16[64,768]{1,0:T(8,128)(2,1)} %tok.1, s32[8,64]{1,0:T(8,128)} %bitcast.8, f32[8,64]{1,0:T(8,128)} %bitcast.9, bf16[4,2,768,128]{3,2,1,0:T(8,128)(2,1)} %bitcast.5, bf16[4,2,768,128]{3,2,1,0:T(8,128)(2,1)} %bitcast.6, bf16[4,2,768,128]{3,2,1,0:T(8,128)(2,1)} %bitcast.7), custom_call_target="tpu_custom_call" | custom-call | flops 603979776 | bytes 4718592 | tf_op jit(solution)/shard_map/experts/pallas_call | solution.py:233
  56.7 1.5 %copy.8 = bf16[64,768]{1,0:T(8,128)(2,1)} copy(bf16[64,768]{1,0:T(8,128)(2,1)} %experts.1) | data formatting | bytes 196608

commit v5 on v4

--- a/solution.py
+++ b/solution.py
@@ -32,11 +32,17 @@
 
 
 def kernel(
-    tok, ids, rw, wg_hbm, wu_hbm, wd_hbm, out,
-    wgu, wd, flat, osend, orecv, xall, part, other, rsend, rrecv, mine, dsend, drecv, mixed,
-    w_sem, w_ssem, w_rsem, column_sem, o_ssem, o_rsem, x_ssem, x_rsem, p_ssem, p_rsem,
+    tok_hbm, ids_hbm, rw_hbm, wg_hbm, wu_hbm, wd_hbm, out,
+    tok, ids, rw, wgu, wd, flat, osend, orecv, xall, part, other, rsend, rrecv, mine, dsend, drecv, mixed,
+    in_sem, w_sem, w_ssem, w_rsem, column_sem, o_ssem, o_rsem, x_ssem, x_rsem, p_ssem, p_rsem,
     r_ssem, r_rsem, d_ssem, d_rsem,
 ):
+    inputs = [
+        pltpu.make_async_copy(src, dst, in_sem.at[i])
+        for i, (src, dst) in enumerate(((ids_hbm, ids), (rw_hbm, rw), (tok_hbm, tok)))
+    ]
+    for copy in inputs:
+        copy.start()
     e, w = lax.axis_index("expert"), lax.axis_index("width")
     y, z = e // Z, e % Z
     x, core = w // 2, w % 2
@@ -95,6 +101,8 @@
         flat[pl.ds(0, n * TILES), :] = rows.astype(F32).reshape(n * TILES, LANES)
         return jnp.concatenate([flat[pl.ds(j, n, TILES), :].astype(BF16) for j in range(TILES)], axis=1)
 
+    for copy in inputs:
+        copy.wait()
     expert = iota((ALL, TOK), 0)
     match = jnp.zeros((ALL, TOK), F32)
     weight = jnp.zeros((ALL, TOK), F32)
@@ -104,12 +112,8 @@
         weight = jnp.where(hit, rw[k : k + 1, :], weight)
     earlier = jnp.where(iota((TOK, TOK), 0) < iota((TOK, TOK), 1), 1.0, 0.0).astype(BF16)
     rank = dot(match.astype(BF16), earlier)
-    coeffs = []
-    for q in range(Q):
-        chosen = jnp.where(rank == float(q), match, 0.0)
-        high = (weight * chosen).astype(BF16)
-        coeffs.append((high, (weight * chosen - high.astype(F32)).astype(BF16)))
-        osend[q] = fold(dot(chosen.astype(BF16), tok[...]))
+    chosen = [jnp.where(rank == float(q), match, 0.0) for q in range(Q)]
+    osend[0] = fold(dot(chosen[0].astype(BF16), tok[...]))
 
     pl.semaphore_wait(bar, len(near) + len(around) + 1)
 
@@ -195,14 +199,21 @@
             out[...] = total.astype(BF16)
 
     column_is_in()
-    for k in range(K):
-        out_to(k, near)
+    out_to(0, near)
+    out_to(1, near)
+    osend[1] = fold(dot(chosen[1].astype(BF16), tok[...]))
+    out_to(2, near)
+    out_to(3, near)
     columns_are_in()
     for k in range(K):
         out_to(k, far)
         if k % 2 == 0:
             out_own(k // 2)
     start_weights()
+    coeffs = []
+    for q in range(Q):
+        high = (weight * chosen[q]).astype(BF16)
+        coeffs.append((high, (weight * chosen[q] - high.astype(F32)).astype(BF16)))
     for k in range(K):
         out_x(k)
     weights_here()
@@ -233,9 +244,12 @@
     return pl.pallas_call(
         kernel,
         out_shape=jax.ShapeDtypeStruct((TOK, FEAT), BF16),
-        in_specs=[vmem, vmem, vmem, hbm, hbm, hbm],
+        in_specs=[hbm] * 6,
         out_specs=vmem,
         scratch_shapes=[
+            pltpu.VMEM((TOK, FEAT), BF16),
+            pltpu.VMEM(expert_ids.T.shape, jnp.int32),
+            pltpu.VMEM(route_weight.T.shape, F32),
             pltpu.VMEM((X, FEAT, 2 * CHIP), BF16),
             pltpu.VMEM((X, FEAT, CHIP), BF16),
             pltpu.VMEM((ALL * TILES, LANES), F32),
@@ -250,7 +264,7 @@
             pltpu.VMEM((K, ROWS, *lying), BF16),
             pltpu.VMEM((Q, ALL, *lying), BF16),
             pltpu.VMEM((TOK, FEAT), F32),
-            dma((3,)), dma((3,)), dma((3,)), pltpu.SemaphoreType.REGULAR,
+            dma((3,)), dma((3,)), dma((3,)), dma((3,)), pltpu.SemaphoreType.REGULAR,
             dma, dma((K,)), dma, dma((K, X - 1)), dma, dma((K,)),
             dma, dma((K, X - 1)), dma, dma((Q,)),
         ],

time: 58.4 us -> 57.7 us (0.988)
  Pallas kernels: 56.7 us -> 55.9 us
    pallas_call x1, Pallas kernels: 56.7 us -> 55.9 us  [body(): pl.pallas_call(kernel, out_shape=jax.ShapeDtypeStruct((TOK, FEAT), BF16),...]
where the time goes in v5:
time: 57.7 us; the launch traced here: 57.5 us
  Pallas kernels  55.9 us (97%)
  local copies, waits for them, and re-layouts  1.54 us (3%)
    pallas_call x1, Pallas kernels, body(): pl.pallas_call(kernel, out_shape=jax.ShapeDtypeStruct((TOK, FEAT), BF16),...  55.9 us
    unnamed x1, local copies, waits for them, and re-layouts  1.54 us

profile of v5, /device:TPU:33, one launch (start us, length us, event | category | flops | bytes accessed | tf_op | source)
XLA Modules:
  0.0 57.5 jit_solution(15418808306298033705)
XLA Ops:
  0.0 55.9 %experts.1 = bf16[64,768]{1,0:T(8,128)(2,1)} custom-call(bf16[64,768]{1,0:T(8,128)(2,1)} %tok_hbm.1, s32[8,64]{1,0:T(8,128)} %bitcast.8, f32[8,64]{1,0:T(8,128)} %bitcast.9, bf16[4,2,768,128]{3,2,1,0:T(8,128)(2,1)} %bitcast.5, bf16[4,2,768,128]{3,2,1,0:T(8,128)(2,1)} %bitcast.6, bf16[4,2,768,128]{3,2,1,0:T(8,128)(2,1)} %bitcast.7), custom_call_target="tpu_custom_call" | custom-call | flops 603979776 | bytes 4718592 | tf_op jit(solution)/shard_map/experts/pallas_call | solution.py:244
  55.9 1.5 %copy.8 = bf16[64,768]{1,0:T(8,128)(2,1)} copy(bf16[64,768]{1,0:T(8,128)(2,1)} %experts.1) | data formatting | bytes 196608

commit v6 on v5

--- a/solution.py
+++ b/solution.py
@@ -48,7 +48,7 @@
     x, core = w // 2, w % 2
     partner = x * 2 + (1 - core)
     xl, xr, xo = (x + X - 1) % X, (x + 1) % X, (x + 2) % X
-    around = [xo, xr, xl]
+    around = [xr, xl, xo]
     yorder = [2, 1, 3]
     zorder = [8, 7, 9, 6, 10, 5, 11, 4, 12, 3, 13, 2, 14, 1, 15]
 
@@ -83,6 +83,8 @@
     for xx in around:
         greet(e, xx * 2 + core)
     greet(e, partner)
+    for dy, dz in far:
+        greet(peer(dy, dz), w)
 
     def remote(src, dst, ssem, rsem, ee, ww):
         pltpu.make_async_remote_copy(
@@ -115,7 +117,7 @@
     chosen = [jnp.where(rank == float(q), match, 0.0) for q in range(Q)]
     osend[0] = fold(dot(chosen[0].astype(BF16), tok[...]))
 
-    pl.semaphore_wait(bar, len(near) + len(around) + 1)
+    pl.semaphore_wait(bar, len(near) + len(far) + len(around) + 1)
 
     def column_is_in():
         for dy in yorder:
@@ -158,7 +160,7 @@
 
     def gathered(k):
         total = project(k, x)
-        for i, xx in ((1, xl), (2, xr), (0, xo)):
+        for i, xx in ((0, xl), (1, xr), (2, xo)):
             wait_bytes(xall.at[k, xx], x_rsem.at[k, i])
             total = total + project(k, xx)
         part[k] = total
@@ -176,7 +178,7 @@
 
     def back(k):
         total = mine[k]
-        for i in (1, 2, 0):
+        for i in (0, 1, 2):
             wait_bytes(rrecv.at[k, i], r_rsem.at[k, i])
             total = total + rrecv[k, i].astype(F32)
         dsend[k] = fold(total)
@@ -198,17 +200,13 @@
         else:
             out[...] = total.astype(BF16)
 
-    column_is_in()
-    out_to(0, near)
-    out_to(1, near)
+    out_to(0, far + near)
+    out_own(0)
+    out_to(1, far + near)
     osend[1] = fold(dot(chosen[1].astype(BF16), tok[...]))
-    out_to(2, near)
-    out_to(3, near)
-    columns_are_in()
-    for k in range(K):
-        out_to(k, far)
-        if k % 2 == 0:
-            out_own(k // 2)
+    out_to(2, far + near)
+    out_own(1)
+    out_to(3, far + near)
     start_weights()
     coeffs = []
     for q in range(Q):

time: 57.7 us -> 57.4 us (level)
  no operation moved by 1% of the time
where the time goes in v6:
time: 57.4 us; the launch traced here: 57.3 us
  Pallas kernels  55.7 us (97%)
  local copies, waits for them, and re-layouts  1.54 us (3%)
    pallas_call x1, Pallas kernels, body(): pl.pallas_call(kernel, out_shape=jax.ShapeDtypeStruct((TOK, FEAT), BF16),...  55.7 us
    unnamed x1, local copies, waits for them, and re-layouts  1.54 us

profile of v6, /device:TPU:33, one launch (start us, length us, event | category | flops | bytes accessed | tf_op | source)
XLA Modules:
  0.0 57.3 jit_solution(11451723042658731796)
XLA Ops:
  0.0 55.7 %experts.1 = bf16[64,768]{1,0:T(8,128)(2,1)} custom-call(bf16[64,768]{1,0:T(8,128)(2,1)} %tok_hbm.1, s32[8,64]{1,0:T(8,128)} %bitcast.8, f32[8,64]{1,0:T(8,128)} %bitcast.9, bf16[4,2,768,128]{3,2,1,0:T(8,128)(2,1)} %bitcast.5, bf16[4,2,768,128]{3,2,1,0:T(8,128)(2,1)} %bitcast.6, bf16[4,2,768,128]{3,2,1,0:T(8,128)(2,1)} %bitcast.7), custom_call_target="tpu_custom_call" | custom-call | flops 603979776 | bytes 4718592 | tf_op jit(solution)/shard_map/experts/pallas_call | solution.py:242
  55.7 1.5 %copy.8 = bf16[64,768]{1,0:T(8,128)(2,1)} copy(bf16[64,768]{1,0:T(8,128)(2,1)} %experts.1) | data formatting | bytes 196608
